TPU v7x, 256 devices: a whole 4x4x8 slice. The times are simulated.
256 devices in a mesh: dp: 16 (over y_lo, x, core), seq: 16 (over z, y_hi).
Axes of the slice: x: 4, y: 4 (y_hi: 2, y_lo: 2; y = y_hi * 2 + y_lo), z: 8, core: 2. Of those that a mesh axis runs over, the one named last changes fastest.
Arguments:
- primal: bfloat16 [16, 2048, 3, 4096], P('dp', 'seq'), as said below
- tangent: bfloat16 [16, 2048, 3, 4096], P('dp', 'seq'), may hold values from -6 to 6
- cotangent: bfloat16 [16, 2048, 2560], P('dp', 'seq'), may hold values from -6 to 6
Outputs:
- attended: bfloat16 [16, 2048, 4096], P('dp', 'seq')
- attended_tangent: bfloat16 [16, 2048, 4096], P('dp', 'seq')
- weight_grad: float32 [2560, 4096], P('dp', 'seq')
Inputs may be any that keep to these rules, and one draw needn't show every extreme that they name: `primal`: slots 0, 1, 2 of the third dimension are queries, keys and values.
All inputs are finite; a program needn't handle non-finite values.
Results may differ from a plain program's by a relative error of at most 0.005.
Values may be sent and summed in bfloat16 or wider, within the bound.
A program may use at most 128 MiB of HBM per device.

v0:
```python
import jax
import jax.numpy as jnp
from jax import lax
from jax.sharding import PartitionSpec as P

HEAD_DIM = 128


def block_jvp(query_block, dquery_block, keys, dkeys, values, dvalues):
    scale = 1.0 / HEAD_DIM**0.5
    scores = (
        jnp.einsum("qhd,khd->hqk", query_block, keys, preferred_element_type=jnp.float32) * scale
    )
    top = jnp.max(scores, axis=-1, keepdims=True)
    expo = jnp.exp(scores - top)
    probs = expo / jnp.sum(expo, axis=-1, keepdims=True)
    probs_low = probs.astype(jnp.bfloat16)
    out = jnp.einsum("hqk,khd->qhd", probs_low, values, preferred_element_type=jnp.float32)
    dscores = jnp.einsum("qhd,khd->hqk", dquery_block, keys, preferred_element_type=jnp.float32)
    dscores = (
        dscores + jnp.einsum("qhd,khd->hqk", query_block, dkeys, preferred_element_type=jnp.float32)
    ) * scale
    centre = jnp.sum(probs * dscores, axis=-1, keepdims=True)
    dprobs = (probs * (dscores - centre)).astype(jnp.bfloat16)
    dout = jnp.einsum("hqk,khd->qhd", probs_low, dvalues, preferred_element_type=jnp.float32)
    dout = dout + jnp.einsum("hqk,khd->qhd", dprobs, values, preferred_element_type=jnp.float32)
    return (out.astype(jnp.bfloat16), dout.astype(jnp.bfloat16))


def body(primal, tangent, cotangent):
    prim_heads, tang_heads = (
        lax.all_to_all(primal, "seq", split_axis=3, concat_axis=1, tiled=True),
        lax.all_to_all(tangent, "seq", split_axis=3, concat_axis=1, tiled=True),
    )
    seq_len = prim_heads.shape[1]
    local_width = prim_heads.shape[3]
    head_count = local_width // HEAD_DIM
    prim_heads = prim_heads[0].reshape(seq_len, 3, head_count, HEAD_DIM)
    tang_heads = tang_heads[0].reshape(seq_len, 3, head_count, HEAD_DIM)
    keys, values = (prim_heads[:, 1], prim_heads[:, 2])
    dkeys, dvalues = (tang_heads[:, 1], tang_heads[:, 2])
    block = min(512, seq_len)
    queries = prim_heads[:, 0].reshape(seq_len // block, block, head_count, HEAD_DIM)
    dqueries = tang_heads[:, 0].reshape(seq_len // block, block, head_count, HEAD_DIM)

    def one_block(pair):
        return block_jvp(pair[0], pair[1], keys, dkeys, values, dvalues)

    outs, douts = lax.map(one_block, (queries, dqueries))
    outs = outs.reshape(1, seq_len, local_width)
    douts = douts.reshape(1, seq_len, local_width)
    attended, attended_tangent = (
        lax.all_to_all(outs, "seq", split_axis=1, concat_axis=2, tiled=True),
        lax.all_to_all(douts, "seq", split_axis=1, concat_axis=2, tiled=True),
    )
    full_cot = lax.all_gather(cotangent, "seq", axis=1, tiled=True)[0]
    heads_out = outs[0]
    term = lax.dot_general(
        full_cot, heads_out, (((0,), (0,)), ((), ())), preferred_element_type=jnp.float32
    )
    weight_grad = lax.psum_scatter(term, "dp", scatter_dimension=0, tiled=True)
    return (attended, attended_tangent, weight_grad)


def solution(mesh):
    return jax.shard_map(
        body,
        mesh=mesh,
        in_specs=(P("dp", "seq", None, None), P("dp", "seq", None, None), P("dp", "seq", None)),
        out_specs=(P("dp", "seq", None), P("dp", "seq", None), P("dp", "seq")),
        check_vma=False,
    )
```

profile of v0, /device:TPU:6, one launch (start us, length us, event | category | flops | bytes accessed | tf_op | source)
XLA Modules:
  0.0 478.7 jit_solution(12705735730795649485)
XLA Ops:
  7.2 7.3 %copy.42 = bf16[1,128,3,4096]{1,2,0,3:T(4,128)(2,1)} copy(bf16[1,128,3,4096]{3,1,2,0:T(8,128)(2,1)} %param.6) | data formatting | bytes 6291456 | tf_op args[1]
  14.5 11.3 %all-to-all-start.1 = ((bf16[1,128,3,4096]{1,2,0,3:T(4,128)(2,1)}), bf16[1,128,3,4096]{1,2,0,3:T(4,128)(2,1)}, u32[]{:S(2)}, u32[]{:S(2)}) async-start(bf16[1,128,3,4096]{1,2,0,3:T(4,128)(2,1)} %copy.42), calls=%async_computation.1 | async-start | bytes 8388608 | tf_op jit(solution)/shard_map/all_to_all | solution.py:33
  25.8 4.8 copy.39
  30.5 94.0 %all-to-all-done.1 = bf16[1,128,3,4096]{1,2,0,3:T(4,128)(2,1)} async-done(((bf16[1,128,3,4096]{1,2,0,3:T(4,128)(2,1)}), bf16[1,128,3,4096]{1,2,0,3:T(4,128)(2,1)}, u32[]{:S(2)}, u32[]{:S(2)}) %all-to-all-start.1) | async-done | bytes 3145760 | tf_op jit(solution)/shard_map/all_to_all | solution.py:33
  124.6 5.2 %all-to-all-start = ((bf16[1,128,3,4096]{1,2,0,3:T(4,128)(2,1)}), bf16[1,128,3,4096]{1,2,0,3:T(4,128)(2,1)}, u32[]{:S(2)}, u32[]{:S(2)}) async-start(bf16[1,128,3,4096]{1,2,0,3:T(4,128)(2,1)} %copy.39), calls=%async_computation | async-start | bytes 8388608 | tf_op jit(solution)/shard_map/all_to_all | solution.py:32
  130.6 4.8 copy.80
  143.5 105.6 %all-to-all-done = bf16[1,128,3,4096]{1,2,0,3:T(4,128)(2,1)} async-done(((bf16[1,128,3,4096]{1,2,0,3:T(4,128)(2,1)}), bf16[1,128,3,4096]{1,2,0,3:T(4,128)(2,1)}, u32[]{:S(2)}, u32[]{:S(2)}) %all-to-all-start) | async-done | bytes 3145760 | tf_op jit(solution)/shard_map/all_to_all | solution.py:32
  249.1 4.8 copy.81
  270.1 99.2 %while.12 = (s32[]{:T(128)}, bf16[4,512,2,128]{3,2,1,0:T(2,128)(2,1)S(1)}, bf16[4,512,2,128]{3,2,1,0:T(2,128)(2,1)}, bf16[4,512,2,128]{3,1,0,2:T(8,128)(2,1)}, b...) while((s32[]{:T(128)}, ...), condition=%wide.region_4.5_spmd, body=%wide.region_0.4_spmd.sunk | while | flops 3255174144 | bytes 131365072 | solution.py:49
  270.1 6.9 %fusion.95 = (f32[2,512]{1,0:T(2,128)S(1)}, f32[2,512,2048]{2,1,0:T(8,128)}) fusion(bf16[2048,2,128]{2,0,1:T(8,128)(2,1)S(1)} %get-tuple-element.213, bf16[4,512,2,128]{3,1,0,2:T(8,128)(2,1)} %get-tuple-element.212, s32[]{:T(128)} %get-tuple-element.199), kind=kOutput, calls=%fused_computation.49.clone.1 | convolution fusion | flops 543164416 | bytes 9703936 | tf_op jit(solution)/shard_map/while/body/eval_jaxpr/sub | solution.py:15
  280.7 5.5 %multiply_reduce_fusion.3 = (f32[2,512]{1,0:T(2,128)S(1)}, f32[2,512,2048]{2,1,0:T(8,128)}) fusion(f32[2,512,2048]{2,1,0:T(8,128)S(1)} %copy-done.7, f32[2,512]{1,0:T(2,128)S(1)} %get-tuple-element.184, f32[2,512,2048]{2,1,0:T(8,128)S(1)} %fusion.96, bf16[2048,2,128]{2,0,1:T(8,128)(2,1)S(1)} %copy-done.6, ...), kind=kOutput, calls=%fused_computation.2.clone.1 | convolution fusion | flops 547355648 | bytes 26485248 | tf_op jit(solution)/shard_map/while/body/eval_jaxpr/qhd,khd->hqk/dot_general | solution.py:21
  294.8 6.9 %fusion.95 = (f32[2,512]{1,0:T(2,128)S(1)}, f32[2,512,2048]{2,1,0:T(8,128)}) fusion(bf16[2048,2,128]{2,0,1:T(8,128)(2,1)S(1)} %get-tuple-element.213, bf16[4,512,2,128]{3,1,0,2:T(8,128)(2,1)} %get-tuple-element.212, s32[]{:T(128)} %get-tuple-element.199), kind=kOutput, calls=%fused_computation.49.clone.1 | convolution fusion | flops 543164416 | bytes 9703936 | tf_op jit(solution)/shard_map/while/body/eval_jaxpr/sub | solution.py:15
  305.5 5.5 %multiply_reduce_fusion.3 = (f32[2,512]{1,0:T(2,128)S(1)}, f32[2,512,2048]{2,1,0:T(8,128)}) fusion(f32[2,512,2048]{2,1,0:T(8,128)S(1)} %copy-done.7, f32[2,512]{1,0:T(2,128)S(1)} %get-tuple-element.184, f32[2,512,2048]{2,1,0:T(8,128)S(1)} %fusion.96, bf16[2048,2,128]{2,0,1:T(8,128)(2,1)S(1)} %copy-done.6, ...), kind=kOutput, calls=%fused_computation.2.clone.1 | convolution fusion | flops 547355648 | bytes 26485248 | tf_op jit(solution)/shard_map/while/body/eval_jaxpr/qhd,khd->hqk/dot_general | solution.py:21
  319.6 6.9 %fusion.95 = (f32[2,512]{1,0:T(2,128)S(1)}, f32[2,512,2048]{2,1,0:T(8,128)}) fusion(bf16[2048,2,128]{2,0,1:T(8,128)(2,1)S(1)} %get-tuple-element.213, bf16[4,512,2,128]{3,1,0,2:T(8,128)(2,1)} %get-tuple-element.212, s32[]{:T(128)} %get-tuple-element.199), kind=kOutput, calls=%fused_computation.49.clone.1 | convolution fusion | flops 543164416 | bytes 9703936 | tf_op jit(solution)/shard_map/while/body/eval_jaxpr/sub | solution.py:15
  330.3 5.6 %multiply_reduce_fusion.3 = (f32[2,512]{1,0:T(2,128)S(1)}, f32[2,512,2048]{2,1,0:T(8,128)}) fusion(f32[2,512,2048]{2,1,0:T(8,128)S(1)} %copy-done.7, f32[2,512]{1,0:T(2,128)S(1)} %get-tuple-element.184, f32[2,512,2048]{2,1,0:T(8,128)S(1)} %fusion.96, bf16[2048,2,128]{2,0,1:T(8,128)(2,1)S(1)} %copy-done.6, ...), kind=kOutput, calls=%fused_computation.2.clone.1 | convolution fusion | flops 547355648 | bytes 26485248 | tf_op jit(solution)/shard_map/while/body/eval_jaxpr/qhd,khd->hqk/dot_general | solution.py:21
  344.5 6.9 %fusion.95 = (f32[2,512]{1,0:T(2,128)S(1)}, f32[2,512,2048]{2,1,0:T(8,128)}) fusion(bf16[2048,2,128]{2,0,1:T(8,128)(2,1)S(1)} %get-tuple-element.213, bf16[4,512,2,128]{3,1,0,2:T(8,128)(2,1)} %get-tuple-element.212, s32[]{:T(128)} %get-tuple-element.199), kind=kOutput, calls=%fused_computation.49.clone.1 | convolution fusion | flops 543164416 | bytes 9703936 | tf_op jit(solution)/shard_map/while/body/eval_jaxpr/sub | solution.py:15
  355.2 5.5 %multiply_reduce_fusion.3 = (f32[2,512]{1,0:T(2,128)S(1)}, f32[2,512,2048]{2,1,0:T(8,128)}) fusion(f32[2,512,2048]{2,1,0:T(8,128)S(1)} %copy-done.7, f32[2,512]{1,0:T(2,128)S(1)} %get-tuple-element.184, f32[2,512,2048]{2,1,0:T(8,128)S(1)} %fusion.96, bf16[2048,2,128]{2,0,1:T(8,128)(2,1)S(1)} %copy-done.6, ...), kind=kOutput, calls=%fused_computation.2.clone.1 | convolution fusion | flops 547355648 | bytes 26485248 | tf_op jit(solution)/shard_map/while/body/eval_jaxpr/qhd,khd->hqk/dot_general | solution.py:21
  370.2 5.9 %fusion.53 = f32[2560,256]{0,1:T(8,128)S(1)} fusion(bf16[1,2048,2560]{2,1,0:T(8,128)(2,1)} %all-gather.2.cloned.1.call-done, bf16[256,8,2,128]{3,2,1,0:T(2,128)(2,1)} %bitcast.118), kind=kOutput, calls=%fused_computation.40 | convolution fusion | flops 2684354560 | bytes 14155776 | tf_op jit(solution)/shard_map/dot_general | solution.py:58
  378.3 6.4 %reshape.19 = bf16[1,2048,256]{2,0,1:T(2,128)(2,1)S(1)} reshape(bf16[4,512,2,128]{3,2,1,0:T(2,128)(2,1)} %copy-done.1) | data formatting | bytes 2097152 | tf_op jit(solution)/shard_map/reshape | solution.py:50
  385.2 10.7 %reduce = bf16[2048,256]{1,0:T(8,128)(2,1)S(1)} reduce(bf16[2048,1,256]{2,1,0:T(2,128)(2,1)S(1)} %bitcast.116, bf16[]{:T(256)} %broadcast.18), dimensions={1}, to_apply=%bitcast.71.reduce_sub_computation | reduce | bytes 2097154
  401.7 6.4 %reshape.20 = bf16[1,2048,256]{2,0,1:T(2,128)(2,1)S(1)} reshape(bf16[4,512,2,128]{3,2,1,0:T(2,128)(2,1)} %get-tuple-element.52) | data formatting | bytes 2097152 | tf_op jit(solution)/shard_map/reshape | solution.py:51
  408.1 11.5 %reduce.1 = bf16[2048,256]{1,0:T(8,128)(2,1)} reduce(bf16[2048,1,256]{2,1,0:T(2,128)(2,1)S(1)} %bitcast.117, bf16[]{:T(256)} %broadcast.18), dimensions={1}, to_apply=%bitcast.73.reduce_sub_computation | reduce | bytes 2097154
  421.8 10.0 %all-to-all-done.2 = bf16[16,2,16384]{2,1,0:T(2,128)(2,1)S(1)} async-done(((bf16[16,2,16384]{2,1,0:T(2,128)(2,1)}), bf16[16,2,16384]{2,1,0:T(2,128)(2,1)S(1)}, u32[]{:S(2)}, u32[]{:S(2)}) %all-to-all-start.2) | async-done | bytes 1048608 | tf_op jit(solution)/shard_map/all_to_all | solution.py:53
  439.4 25.9 %all-to-all-done.3 = bf16[16,2,16384]{2,1,0:T(2,128)(2,1)} async-done(((bf16[16,2,16384]{2,1,0:T(2,128)(2,1)}), bf16[16,2,16384]{2,1,0:T(2,128)(2,1)}, u32[]{:S(2)}, u32[]{:S(2)}) %all-to-all-start.3) | async-done | bytes 1048608 | tf_op jit(solution)/shard_map/all_to_all | solution.py:54
  (92 shorter events, 100.3 us)
Async XLA Ops:
  7.2 18.6 %copy-start.3 = (bf16[1,128,3,4096]{3,1,2,0:T(8,128)(2,1)S(1)}, bf16[1,128,3,4096]{3,1,2,0:T(8,128)(2,1)}, u32[]{:S(2)}) copy-start(bf16[1,128,3,4096]{3,1,2,0:T(8,128)(2,1)} %param.5) | copy-start | bytes 9437188
  14.5 110.1 %all-to-all-start.1 = ((bf16[1,128,3,4096]{1,2,0,3:T(4,128)(2,1)}), bf16[1,128,3,4096]{1,2,0,3:T(4,128)(2,1)}, u32[]{:S(2)}, u32[]{:S(2)}) async-start(bf16[1,128,3,4096]{1,2,0,3:T(4,128)(2,1)} %copy.42), calls=%async_computation.1 | async-start | bytes 8388608 | tf_op jit(solution)/shard_map/all_to_all | solution.py:33
  124.6 124.5 %all-to-all-start = ((bf16[1,128,3,4096]{1,2,0,3:T(4,128)(2,1)}), bf16[1,128,3,4096]{1,2,0,3:T(4,128)(2,1)}, u32[]{:S(2)}, u32[]{:S(2)}) async-start(bf16[1,128,3,4096]{1,2,0,3:T(4,128)(2,1)} %copy.39), calls=%async_computation | async-start | bytes 8388608 | tf_op jit(solution)/shard_map/all_to_all | solution.py:32
  129.8 239.5 %all-gather.2.cloned.1.call-start = ((), (), s32[]{:S(2)}) async-start(), calls=%async_computation.5 | async-start | bytes 11141120 | tf_op jit(solution)/shard_map/all_gather | solution.py:56
  130.5 341.3 %reduce-scatter.4.cloned.1.call-start = ((), (), s32[]{:S(2)}) async-start(), calls=%async_computation.6 | async-start | bytes 2785280
  257.2 11.5 %copy-start.2 = (bf16[2048,2,128]{0,2,1:T(8,128)(2,1)S(1)}, bf16[2048,2,128]{0,2,1:T(8,128)(2,1)}, u32[]{:S(2)}) copy-start(bf16[2048,2,128]{0,2,1:T(8,128)(2,1)} %get-tuple-element.116) | copy-start | bytes 3145732
  257.2 12.8 %copy-start = (bf16[4,512,2,128]{3,2,1,0:T(2,128)(2,1)S(1)}, bf16[4,512,2,128]{3,2,1,0:T(2,128)(2,1)}, u32[]{:S(2)}) copy-start(bf16[4,512,2,128]{3,2,1,0:T(2,128)(2,1)} %custom-call) | copy-start | bytes 3145732
  276.9 2.4 copy-start.6
  276.9 3.8 copy-start.7
  280.7 5.5 %copy-start.4 = (bf16[2048,2,128]{2,0,1:T(8,128)(2,1)S(1)}, bf16[2048,2,128]{2,0,1:T(8,128)(2,1)}, u32[]{:S(2)}) copy-start(bf16[2048,2,128]{2,0,1:T(8,128)(2,1)} %get-tuple-element.214) | copy-start | bytes 3145732 | tf_op jit(solution)/shard_map/while
  286.2 4.5 copy-start.5
  301.6 2.4 copy-start.6
  301.6 3.9 copy-start.7
  305.5 5.5 %copy-start.4 = (bf16[2048,2,128]{2,0,1:T(8,128)(2,1)S(1)}, bf16[2048,2,128]{2,0,1:T(8,128)(2,1)}, u32[]{:S(2)}) copy-start(bf16[2048,2,128]{2,0,1:T(8,128)(2,1)} %get-tuple-element.214) | copy-start | bytes 3145732 | tf_op jit(solution)/shard_map/while
  311.0 4.5 copy-start.5
  326.4 2.4 copy-start.6
  326.4 3.9 copy-start.7
  330.3 5.6 %copy-start.4 = (bf16[2048,2,128]{2,0,1:T(8,128)(2,1)S(1)}, bf16[2048,2,128]{2,0,1:T(8,128)(2,1)}, u32[]{:S(2)}) copy-start(bf16[2048,2,128]{2,0,1:T(8,128)(2,1)} %get-tuple-element.214) | copy-start | bytes 3145732 | tf_op jit(solution)/shard_map/while
  335.9 4.6 copy-start.5
  351.4 3.8 copy-start.7
  355.2 5.5 %copy-start.4 = (bf16[2048,2,128]{2,0,1:T(8,128)(2,1)S(1)}, bf16[2048,2,128]{2,0,1:T(8,128)(2,1)}, u32[]{:S(2)}) copy-start(bf16[2048,2,128]{2,0,1:T(8,128)(2,1)} %get-tuple-element.214) | copy-start | bytes 3145732 | tf_op jit(solution)/shard_map/while
  360.7 4.5 copy-start.5
  397.1 34.7 %all-to-all-start.2 = ((bf16[16,2,16384]{2,1,0:T(2,128)(2,1)}), bf16[16,2,16384]{2,1,0:T(2,128)(2,1)S(1)}, u32[]{:S(2)}, u32[]{:S(2)}) async-start(bf16[16,2,16384]{2,1,0:T(2,128)(2,1)} %reshape.23), calls=%async_computation.2 | async-start | bytes 2097152 | tf_op jit(solution)/shard_map/all_to_all | solution.py:53
  431.8 33.6 %all-to-all-start.3 = ((bf16[16,2,16384]{2,1,0:T(2,128)(2,1)}), bf16[16,2,16384]{2,1,0:T(2,128)(2,1)}, u32[]{:S(2)}, u32[]{:S(2)}) async-start(bf16[16,2,16384]{2,1,0:T(2,128)(2,1)} %reshape.25), calls=%async_computation.3 | async-start | bytes 2097152 | tf_op jit(solution)/shard_map/all_to_all | solution.py:54
  (2 other events, 3.3 us)
Sparse Core Ops, SparseCore 0:
  133.2 223.3 all-gather.1
  378.5 61.9 reduce-scatter.3
where the time goes:
time: 480 us; the launch traced here: 479 us
  waiting for transfers between devices  236 us (49%)
  matrix products  94.1 us (20%)
  local copies, waits for them, and re-layouts  86.2 us (18%)
  starting transfers between devices  25.6 us (5%)
  other arithmetic  22.3 us (5%)
  between operations  14.2 us (3%)
    all_to_all x1, waiting for transfers between devices, body(): lax.all_to_all(primal, 'seq', split_axis=3, concat_axis=1, tiled=True)  106 us
    all_to_all x1, waiting for transfers between devices, body(): lax.all_to_all(tangent, 'seq', split_axis=3, concat_axis=1, tiled=True)  94 us
    sub x4, matrix products, block_jvp(): expo = jnp.exp(scores - top)  27.5 us
    unnamed x20, local copies, waits for them, and re-layouts  27.3 us
    all_to_all x1, waiting for transfers between devices, body(): lax.all_to_all(douts, 'seq', split_axis=1, concat_axis=2, tiled=True)  25.9 us
    unnamed x2, other arithmetic  22.2 us
    dot_general x4, matrix products, block_jvp(): jnp.einsum('qhd,khd->hqk', query_block, dkeys, preferred_element_type=jnp...  22 us
    dot_general x4, matrix products, block_jvp(): jnp.einsum('hqk,khd->qhd', dprobs, values, preferred_element_type=jnp.flo...  18.2 us
  transfers between devices with their start and end apart: 6, of which 4 were waited for; matrix products, arithmetic and copies ran while one was open for 38% of the time, Pallas kernels for 0%

commit v1 on v0

--- a/solution.py
+++ b/solution.py
@@ -30,7 +30,12 @@
 def body(primal, tangent, cotangent):
     prim_heads, tang_heads = (
         lax.all_to_all(primal, "seq", split_axis=3, concat_axis=1, tiled=True),
-        lax.all_to_all(tangent, "seq", split_axis=3, concat_axis=1, tiled=True),
+        jnp.concatenate(
+            lax.all_to_all(
+                jnp.stack(jnp.split(tangent, lax.axis_size("seq"), axis=3)), "seq", 0, 0
+            ),
+            axis=1,
+        ),
     )
     seq_len = prim_heads.shape[1]
     local_width = prim_heads.shape[3]

time: 480 us -> 457 us (0.952)
  waiting for transfers between devices: 236 us -> 207 us
  local copies, waits for them, and re-layouts: 86.2 us -> 92.4 us
    all_to_all x1, waiting for transfers between devices: 94 us -> 67.7 us  [body(): lax.all_to_all(jnp.stack(jnp.split(tangent, lax.axis_size('seq'), axis=3)...]
    unnamed x20 -> x36, local copies, waits for them, and re-layouts: 27.3 us -> 41.6 us
    reshape x1, local copies, waits for them, and re-layouts: 6.36 us -> 0.48 us  [body(): outs = outs.reshape(1, seq_len, local_width)]
where the time goes in v1:
time: 457 us; the launch traced here: 456 us
  waiting for transfers between devices  207 us (45%)
  matrix products  93.8 us (21%)
  local copies, waits for them, and re-layouts  92.4 us (20%)
  starting transfers between devices  25.5 us (6%)
  other arithmetic  22.4 us (5%)
  between operations  14.2 us (3%)
    all_to_all x1, waiting for transfers between devices, body(): lax.all_to_all(primal, 'seq', split_axis=3, concat_axis=1, tiled=True)  103 us
    all_to_all x1, waiting for transfers between devices, body(): lax.all_to_all(jnp.stack(jnp.split(tangent, lax.axis_size('seq'), axis=3)...  67.7 us
    unnamed x36, local copies, waits for them, and re-layouts  41.6 us
    sub x4, matrix products, block_jvp(): expo = jnp.exp(scores - top)  27.4 us
    all_to_all x1, waiting for transfers between devices, body(): lax.all_to_all(douts, 'seq', split_axis=1, concat_axis=2, tiled=True)  25.8 us
    unnamed x2, other arithmetic  22.4 us
    dot_general x4, matrix products, block_jvp(): jnp.einsum('qhd,khd->hqk', query_block, dkeys, preferred_element_type=jnp...  21.8 us
    dot_general x4, matrix products, block_jvp(): jnp.einsum('hqk,khd->qhd', dprobs, values, preferred_element_type=jnp.flo...  18.2 us
  transfers between devices with their start and end apart: 6, of which 4 were waited for; matrix products, arithmetic and copies ran while one was open for 38% of the time, Pallas kernels for 0%

profile of v1, /device:TPU:6, one launch (start us, length us, event | category | flops | bytes accessed | tf_op | source)
XLA Modules:
  0.0 455.9 jit_solution(10449963140685899186)
XLA Ops:
  25.9 11.2 %all-to-all-start.1 = ((bf16[16,1,128,3,256]{4,2,3,1,0:T(8,128)(2,1)}), bf16[16,1,128,3,256]{4,2,3,1,0:T(8,128)(2,1)S(1)}, u32[]{:S(2)}, u32[]{:S(2)}) async-start(bf16[16,1,128,3,256]{4,2,3,1,0:T(8,128)(2,1)} %bitcast_dynamic-update-slice_fusion), calls=%async_computation.1 | async-start | bytes 6291456 | tf_op jit(solution)/shard_map/all_to_all | solution.py:34
  37.1 7.2 %copy.39 = bf16[1,128,3,4096]{1,2,0,3:T(4,128)(2,1)} copy(bf16[1,128,3,4096]{3,1,2,0:T(8,128)(2,1)} %param.5) | data formatting | bytes 6291456 | tf_op args[0]
  44.2 67.7 %all-to-all-done.1 = bf16[16,1,128,3,256]{4,2,3,1,0:T(8,128)(2,1)S(1)} async-done(((bf16[16,1,128,3,256]{4,2,3,1,0:T(8,128)(2,1)}), bf16[16,1,128,3,256]{4,2,3,1,0:T(8,128)(2,1)S(1)}, u32[]{:S(2)}, u32[]{:S(2)}) %all-to-all-start.1) | async-done | bytes 3145760 | tf_op jit(solution)/shard_map/all_to_all | solution.py:34
  112.0 4.6 all-to-all-start
  132.7 103.2 %all-to-all-done = bf16[1,128,3,4096]{1,2,0,3:T(4,128)(2,1)} async-done(((bf16[1,128,3,4096]{1,2,0,3:T(4,128)(2,1)}), bf16[1,128,3,4096]{1,2,0,3:T(4,128)(2,1)}, u32[]{:S(2)}, u32[]{:S(2)}) %all-to-all-start) | async-done | bytes 3145760 | tf_op jit(solution)/shard_map/all_to_all | solution.py:32
  235.9 4.8 %copy.78 = bf16[1,128,3,16,256]{1,3,4,2,0:T(8,128)(2,1)S(1)} copy(bf16[1,128,3,16,256]{1,2,4,3,0:T(4,128)(2,1)} %bitcast.6) | data formatting | bytes 6291456 | tf_op jit(solution)/shard_map/all_to_all | solution.py:32
  251.7 98.9 %while.12 = (s32[]{:T(128)}, bf16[4,512,2,128]{3,2,1,0:T(2,128)(2,1)S(1)}, bf16[4,512,2,128]{3,2,1,0:T(2,128)(2,1)}, bf16[4,512,2,128]{3,1,0,2:T(8,128)(2,1)}, b...) while((s32[]{:T(128)}, ...), condition=%wide.region_4.5_spmd, body=%wide.region_0.4_spmd.sunk | while | flops 3255174144 | bytes 131365072 | solution.py:54
  251.7 6.9 %fusion.95 = (f32[2,512]{1,0:T(2,128)S(1)}, f32[2,512,2048]{2,1,0:T(8,128)}) fusion(bf16[2048,2,128]{2,0,1:T(8,128)(2,1)S(1)} %get-tuple-element.213, bf16[4,512,2,128]{3,1,0,2:T(8,128)(2,1)} %get-tuple-element.212, s32[]{:T(128)} %get-tuple-element.199), kind=kOutput, calls=%fused_computation.64.clone.1 | convolution fusion | flops 543164416 | bytes 9703936 | tf_op jit(solution)/shard_map/while/body/eval_jaxpr/sub | solution.py:15
  262.4 5.4 %multiply_reduce_fusion.3 = (f32[2,512]{1,0:T(2,128)S(1)}, f32[2,512,2048]{2,1,0:T(8,128)}) fusion(f32[2,512,2048]{2,1,0:T(8,128)S(1)} %copy-done.8, f32[2,512]{1,0:T(2,128)S(1)} %get-tuple-element.184, f32[2,512,2048]{2,1,0:T(8,128)S(1)} %fusion.96, bf16[2048,2,128]{2,0,1:T(8,128)(2,1)S(1)} %copy-done.6, ...), kind=kOutput, calls=%fused_computation.2.clone.1 | convolution fusion | flops 547355648 | bytes 26485248 | tf_op jit(solution)/shard_map/while/body/eval_jaxpr/qhd,khd->hqk/dot_general | solution.py:21
  276.4 6.9 %fusion.95 = (f32[2,512]{1,0:T(2,128)S(1)}, f32[2,512,2048]{2,1,0:T(8,128)}) fusion(bf16[2048,2,128]{2,0,1:T(8,128)(2,1)S(1)} %get-tuple-element.213, bf16[4,512,2,128]{3,1,0,2:T(8,128)(2,1)} %get-tuple-element.212, s32[]{:T(128)} %get-tuple-element.199), kind=kOutput, calls=%fused_computation.64.clone.1 | convolution fusion | flops 543164416 | bytes 9703936 | tf_op jit(solution)/shard_map/while/body/eval_jaxpr/sub | solution.py:15
  287.0 5.5 %multiply_reduce_fusion.3 = (f32[2,512]{1,0:T(2,128)S(1)}, f32[2,512,2048]{2,1,0:T(8,128)}) fusion(f32[2,512,2048]{2,1,0:T(8,128)S(1)} %copy-done.8, f32[2,512]{1,0:T(2,128)S(1)} %get-tuple-element.184, f32[2,512,2048]{2,1,0:T(8,128)S(1)} %fusion.96, bf16[2048,2,128]{2,0,1:T(8,128)(2,1)S(1)} %copy-done.6, ...), kind=kOutput, calls=%fused_computation.2.clone.1 | convolution fusion | flops 547355648 | bytes 26485248 | tf_op jit(solution)/shard_map/while/body/eval_jaxpr/qhd,khd->hqk/dot_general | solution.py:21
  301.0 6.9 %fusion.95 = (f32[2,512]{1,0:T(2,128)S(1)}, f32[2,512,2048]{2,1,0:T(8,128)}) fusion(bf16[2048,2,128]{2,0,1:T(8,128)(2,1)S(1)} %get-tuple-element.213, bf16[4,512,2,128]{3,1,0,2:T(8,128)(2,1)} %get-tuple-element.212, s32[]{:T(128)} %get-tuple-element.199), kind=kOutput, calls=%fused_computation.64.clone.1 | convolution fusion | flops 543164416 | bytes 9703936 | tf_op jit(solution)/shard_map/while/body/eval_jaxpr/sub | solution.py:15
  311.7 5.5 %multiply_reduce_fusion.3 = (f32[2,512]{1,0:T(2,128)S(1)}, f32[2,512,2048]{2,1,0:T(8,128)}) fusion(f32[2,512,2048]{2,1,0:T(8,128)S(1)} %copy-done.8, f32[2,512]{1,0:T(2,128)S(1)} %get-tuple-element.184, f32[2,512,2048]{2,1,0:T(8,128)S(1)} %fusion.96, bf16[2048,2,128]{2,0,1:T(8,128)(2,1)S(1)} %copy-done.6, ...), kind=kOutput, calls=%fused_computation.2.clone.1 | convolution fusion | flops 547355648 | bytes 26485248 | tf_op jit(solution)/shard_map/while/body/eval_jaxpr/qhd,khd->hqk/dot_general | solution.py:21
  317.2 4.6 %fusion.97 = f32[2,512,128]{2,1,0:T(8,128)S(1)} fusion(bf16[2048,2,128]{2,0,1:T(8,128)(2,1)S(1)} %copy-done.7, f32[2,512,2048]{2,1,0:T(8,128)} %get-tuple-element.185, f32[2,512]{1,0:T(2,128)S(1)} %get-tuple-element.186, f32[2,512,2048]{2,1,0:T(8,128)S(1)} %copy-done.8, f32[2,512]{1,0:T(2,128)S(1)} %get-tuple-element.184), kind=kOutput, calls=%fused_computation.7.clone.1 | convolution fusion | flops 545259520 | bytes 18358272 | tf_op jit(solution)/shard_map/while/body/eval_jaxpr/hqk,khd->qhd/dot_general | solution.py:26
  325.8 6.9 %fusion.95 = (f32[2,512]{1,0:T(2,128)S(1)}, f32[2,512,2048]{2,1,0:T(8,128)}) fusion(bf16[2048,2,128]{2,0,1:T(8,128)(2,1)S(1)} %get-tuple-element.213, bf16[4,512,2,128]{3,1,0,2:T(8,128)(2,1)} %get-tuple-element.212, s32[]{:T(128)} %get-tuple-element.199), kind=kOutput, calls=%fused_computation.64.clone.1 | convolution fusion | flops 543164416 | bytes 9703936 | tf_op jit(solution)/shard_map/while/body/eval_jaxpr/sub | solution.py:15
  336.6 5.4 %multiply_reduce_fusion.3 = (f32[2,512]{1,0:T(2,128)S(1)}, f32[2,512,2048]{2,1,0:T(8,128)}) fusion(f32[2,512,2048]{2,1,0:T(8,128)S(1)} %copy-done.8, f32[2,512]{1,0:T(2,128)S(1)} %get-tuple-element.184, f32[2,512,2048]{2,1,0:T(8,128)S(1)} %fusion.96, bf16[2048,2,128]{2,0,1:T(8,128)(2,1)S(1)} %copy-done.6, ...), kind=kOutput, calls=%fused_computation.2.clone.1 | convolution fusion | flops 547355648 | bytes 26485248 | tf_op jit(solution)/shard_map/while/body/eval_jaxpr/qhd,khd->hqk/dot_general | solution.py:21
  351.5 6.0 %fusion.53 = f32[2560,256]{0,1:T(8,128)S(1)} fusion(bf16[1,2048,2560]{2,1,0:T(8,128)(2,1)} %all-gather.2.cloned.1.call-done, bf16[256,8,2,128]{3,2,1,0:T(2,128)(2,1)} %bitcast.145), kind=kOutput, calls=%fused_computation.40 | convolution fusion | flops 2684354560 | bytes 14155776 | tf_op jit(solution)/shard_map/dot_general | solution.py:63
  361.9 10.8 %reduce = bf16[2048,256]{1,0:T(8,128)(2,1)S(1)} reduce(bf16[2048,1,256]{2,1,0:T(2,128)(2,1)S(1)} %bitcast.143, bf16[]{:T(256)} %broadcast.18), dimensions={1}, to_apply=%bitcast.100.reduce_sub_computation | reduce | bytes 2097154
  373.8 4.9 %all-to-all-start.2 = ((bf16[16,2,16384]{2,1,0:T(2,128)(2,1)}), bf16[16,2,16384]{2,1,0:T(2,128)(2,1)S(1)}, u32[]{:S(2)}, u32[]{:S(2)}) async-start(bf16[16,2,16384]{2,1,0:T(2,128)(2,1)} %reshape.22), calls=%async_computation.2 | async-start | bytes 2097152 | tf_op jit(solution)/shard_map/all_to_all | solution.py:58
  378.7 6.4 %reshape.19 = bf16[1,2048,256]{2,0,1:T(2,128)(2,1)S(1)} reshape(bf16[4,512,2,128]{3,2,1,0:T(2,128)(2,1)} %get-tuple-element.52) | data formatting | bytes 2097152 | tf_op jit(solution)/shard_map/reshape | solution.py:56
  385.1 11.6 %reduce.1 = bf16[2048,256]{1,0:T(8,128)(2,1)} reduce(bf16[2048,1,256]{2,1,0:T(2,128)(2,1)S(1)} %bitcast.144, bf16[]{:T(256)} %broadcast.18), dimensions={1}, to_apply=%bitcast.102.reduce_sub_computation | reduce | bytes 2097154
  398.8 9.9 %all-to-all-done.2 = bf16[16,2,16384]{2,1,0:T(2,128)(2,1)S(1)} async-done(((bf16[16,2,16384]{2,1,0:T(2,128)(2,1)}), bf16[16,2,16384]{2,1,0:T(2,128)(2,1)S(1)}, u32[]{:S(2)}, u32[]{:S(2)}) %all-to-all-start.2) | async-done | bytes 1048608 | tf_op jit(solution)/shard_map/all_to_all | solution.py:58
  408.7 4.8 %all-to-all-start.3 = ((bf16[16,2,16384]{2,1,0:T(2,128)(2,1)}), bf16[16,2,16384]{2,1,0:T(2,128)(2,1)}, u32[]{:S(2)}, u32[]{:S(2)}) async-start(bf16[16,2,16384]{2,1,0:T(2,128)(2,1)} %reshape.24), calls=%async_computation.3 | async-start | bytes 2097152 | tf_op jit(solution)/shard_map/all_to_all | solution.py:59
  416.7 25.8 %all-to-all-done.3 = bf16[16,2,16384]{2,1,0:T(2,128)(2,1)} async-done(((bf16[16,2,16384]{2,1,0:T(2,128)(2,1)}), bf16[16,2,16384]{2,1,0:T(2,128)(2,1)}, u32[]{:S(2)}, u32[]{:S(2)}) %all-to-all-start.3) | async-done | bytes 1048608 | tf_op jit(solution)/shard_map/all_to_all | solution.py:59
  (109 shorter events, 108.9 us)
Async XLA Ops:
  7.2 13.1 %copy-start.4 = (bf16[1,128,3,4096]{3,1,2,0:T(8,128)(2,1)S(1)}, bf16[1,128,3,4096]{3,1,2,0:T(8,128)(2,1)}, u32[]{:S(2)}) copy-start(bf16[1,128,3,4096]{3,1,2,0:T(8,128)(2,1)} %param.6) | copy-start | bytes 9437188
  25.9 86.1 %all-to-all-start.1 = ((bf16[16,1,128,3,256]{4,2,3,1,0:T(8,128)(2,1)}), bf16[16,1,128,3,256]{4,2,3,1,0:T(8,128)(2,1)S(1)}, u32[]{:S(2)}, u32[]{:S(2)}) async-start(bf16[16,1,128,3,256]{4,2,3,1,0:T(8,128)(2,1)} %bitcast_dynamic-update-slice_fusion), calls=%async_computation.1 | async-start | bytes 6291456 | tf_op jit(solution)/shard_map/all_to_all | solution.py:34
  112.0 124.0 %all-to-all-start = ((bf16[1,128,3,4096]{1,2,0,3:T(4,128)(2,1)}), bf16[1,128,3,4096]{1,2,0,3:T(4,128)(2,1)}, u32[]{:S(2)}, u32[]{:S(2)}) async-start(bf16[1,128,3,4096]{1,2,0,3:T(4,128)(2,1)} %copy.39), calls=%async_computation | async-start | bytes 8388608 | tf_op jit(solution)/shard_map/all_to_all | solution.py:32
  116.5 234.0 %all-gather.2.cloned.1.call-start = ((), (), s32[]{:S(2)}) async-start(), calls=%async_computation.5 | async-start | bytes 11141120 | tf_op jit(solution)/shard_map/all_gather | solution.py:61
  117.3 331.8 %reduce-scatter.4.cloned.1.call-start = ((), (), s32[]{:S(2)}) async-start(), calls=%async_computation.6 | async-start | bytes 2785280
  126.8 4.6 %copy-start.3 = (bf16[2048,2,128]{0,2,1:T(8,128)(2,1)S(1)}, bf16[2048,2,128]{0,2,1:T(8,128)(2,1)}, u32[]{:S(2)}) copy-start(bf16[2048,2,128]{0,2,1:T(8,128)(2,1)} %get-tuple-element.116) | copy-start | bytes 3145732
  247.5 4.2 copy-start
  258.6 3.8 copy-start.8
  262.4 5.4 %copy-start.7 = (bf16[2048,2,128]{2,0,1:T(8,128)(2,1)S(1)}, bf16[2048,2,128]{2,0,1:T(8,128)(2,1)}, u32[]{:S(2)}) copy-start(bf16[2048,2,128]{2,0,1:T(8,128)(2,1)} %get-tuple-element.214) | copy-start | bytes 3145732 | tf_op jit(solution)/shard_map/while
  267.8 4.6 copy-start.5
  283.2 2.4 copy-start.6
  283.2 3.8 copy-start.8
  287.0 5.5 %copy-start.7 = (bf16[2048,2,128]{2,0,1:T(8,128)(2,1)S(1)}, bf16[2048,2,128]{2,0,1:T(8,128)(2,1)}, u32[]{:S(2)}) copy-start(bf16[2048,2,128]{2,0,1:T(8,128)(2,1)} %get-tuple-element.214) | copy-start | bytes 3145732 | tf_op jit(solution)/shard_map/while
  292.5 4.5 copy-start.5
  307.9 2.4 copy-start.6
  307.9 3.8 copy-start.8
  311.7 5.5 %copy-start.7 = (bf16[2048,2,128]{2,0,1:T(8,128)(2,1)S(1)}, bf16[2048,2,128]{2,0,1:T(8,128)(2,1)}, u32[]{:S(2)}) copy-start(bf16[2048,2,128]{2,0,1:T(8,128)(2,1)} %get-tuple-element.214) | copy-start | bytes 3145732 | tf_op jit(solution)/shard_map/while
  317.2 4.6 %copy-start.5 = (bf16[2048,2,128]{2,0,1:T(8,128)(2,1)S(1)}, bf16[2048,2,128]{2,0,1:T(8,128)(2,1)}, u32[]{:S(2)}) copy-start(bf16[2048,2,128]{2,0,1:T(8,128)(2,1)} %get-tuple-element.215) | copy-start | bytes 3145732 | tf_op jit(solution)/shard_map/while
  332.7 2.4 copy-start.6
  332.7 3.9 copy-start.8
  336.6 5.4 %copy-start.7 = (bf16[2048,2,128]{2,0,1:T(8,128)(2,1)S(1)}, bf16[2048,2,128]{2,0,1:T(8,128)(2,1)}, u32[]{:S(2)}) copy-start(bf16[2048,2,128]{2,0,1:T(8,128)(2,1)} %get-tuple-element.214) | copy-start | bytes 3145732 | tf_op jit(solution)/shard_map/while
  342.0 4.5 copy-start.5
  373.8 34.9 %all-to-all-start.2 = ((bf16[16,2,16384]{2,1,0:T(2,128)(2,1)}), bf16[16,2,16384]{2,1,0:T(2,128)(2,1)S(1)}, u32[]{:S(2)}, u32[]{:S(2)}) async-start(bf16[16,2,16384]{2,1,0:T(2,128)(2,1)} %reshape.22), calls=%async_computation.2 | async-start | bytes 2097152 | tf_op jit(solution)/shard_map/all_to_all | solution.py:58
  408.7 33.8 %all-to-all-start.3 = ((bf16[16,2,16384]{2,1,0:T(2,128)(2,1)}), bf16[16,2,16384]{2,1,0:T(2,128)(2,1)}, u32[]{:S(2)}, u32[]{:S(2)}) async-start(bf16[16,2,16384]{2,1,0:T(2,128)(2,1)} %reshape.24), calls=%async_computation.3 | async-start | bytes 2097152 | tf_op jit(solution)/shard_map/all_to_all | solution.py:59
  (3 other events, 4.6 us)
Sparse Core Ops, SparseCore 0:
  120.0 223.5 all-gather.1
  359.8 61.7 reduce-scatter.3
